TPU v7x, 32 devices: a whole 2x2x4 slice. The times are simulated.
32 devices in a mesh: groups: 2 (over y), adapter: 8 (over z, x), tensor: 2 (over core).
Axes of the slice: x: 2, y: 2, z: 4, core: 2. Of those that a mesh axis runs over, the one named last changes fastest.
Arguments:
- hidden: bfloat16 [128, 28672], P(('groups', 'adapter'), 'tensor'), parts along dimension 0, may hold values from -6 to 6
- row_adapter_index: int32 [128, 1], P('groups'), parts along dimension 0, may hold values from 0 to 7; in each aligned block of 64 rows (0 to 63, 64 to 127, ...) at most 16 rows name the same one
- down_matrix: bfloat16 [28672, 8192], P('tensor', 'adapter'), may hold values from -0.03125 to 0.03125
- adapter_input_factor: bfloat16 [8, 28672, 64], P('adapter', 'tensor'), may hold values from -0.03125 to 0.03125
- adapter_output_factor: bfloat16 [8, 64, 8192], P('adapter'), may hold values from -0.75 to 0.75
Outputs:
- mixed: bfloat16 [128, 8192], P('groups', ('adapter', 'tensor')), parts along dimension 0
There are 2 independent parts, one for each index of `groups`. A program takes and returns all parts, laid end to end along the dimension named above; an argument that names none is the same for every part. Nothing has to cross between parts.
Inputs may be any that keep to these rules, and one draw needn't show every extreme that they name: `row_adapter_index`: each of the 8 adapters is named by 1 to 16 rows, a bound that some block reaches.
All inputs are finite; a program needn't handle non-finite values.
Results may differ from a plain program's by a relative error of at most 0.0049.
Values may be sent and summed in bfloat16 or wider, within the bound.
A program may use at most 128 MiB of HBM per device.

v0:
```python
import jax
import jax.numpy as jnp
from jax import lax
from jax.sharding import PartitionSpec as P


def slot_table(row_adapter_index, capacity, adapters):
    idents = row_adapter_index[:, 0]
    onehot = (idents[:, None] == jnp.arange(adapters, dtype=jnp.int32)[None, :]).astype(jnp.int32)
    running = jnp.cumsum(onehot, axis=0) - 1
    ranking = jnp.sum(onehot * running, axis=1)
    return (idents, idents * capacity + ranking)


def on_device(hidden, row_adapter_index, down_matrix, adapter_input_factor, adapter_output_factor):
    adapter_count = lax.axis_size("adapter")
    tensor_count = lax.axis_size("tensor")
    local_row_count, inner_product, adapter_rank_width = adapter_input_factor.shape
    adapters = local_row_count * adapter_count
    rows_total = row_adapter_index.shape[0]
    capacity = 2 * (rows_total // adapter_count) // local_row_count
    idents, slots = slot_table(row_adapter_index, capacity, adapters)
    own_slots = local_row_count * capacity
    first = lax.axis_index("adapter") * own_slots
    wanted = first + jnp.arange(own_slots, dtype=jnp.int32)
    selector = (slots[None, :] == wanted[:, None]).astype(jnp.bfloat16)
    columns = down_matrix.shape[1]
    piece = lax.all_gather(hidden, "adapter", axis=0, tiled=True)
    product = jnp.dot(piece, down_matrix, preferred_element_type=jnp.float32)
    picked = jnp.dot(selector, piece, preferred_element_type=jnp.float32)
    selected_rows = picked.astype(jnp.bfloat16).reshape(local_row_count, capacity, inner_product)
    partial_rank = jnp.einsum(
        "ldm,lmu->ldu", selected_rows, adapter_input_factor, preferred_element_type=jnp.float32
    )
    reduced = lax.psum(partial_rank, "tensor").astype(jnp.bfloat16)
    narrow_hidden = columns // tensor_count
    part_index = lax.axis_index("tensor")
    output_factor_split = adapter_output_factor.reshape(
        local_row_count, adapter_rank_width, adapter_count, tensor_count, narrow_hidden
    )
    b_mine = lax.dynamic_slice_in_dim(output_factor_split, part_index, 1, 3)[:, :, :, 0, :]
    produced = jnp.einsum(
        "ask,akjc->jasc", reduced, b_mine, preferred_element_type=jnp.float32
    ).astype(jnp.bfloat16)
    produced = produced.reshape(adapter_count, own_slots * narrow_hidden)
    arrived = lax.all_to_all(produced, "adapter", split_axis=0, concat_axis=0, tiled=True).reshape(
        adapters * capacity, narrow_hidden
    )
    delta = jnp.take(arrived, slots, axis=0)
    summed = lax.psum_scatter(product, "tensor", scatter_dimension=1, tiled=True)
    return (summed + delta.astype(jnp.float32)).astype(jnp.bfloat16)


def solution(mesh):
    in_specs = (
        P(("groups", "adapter"), "tensor"),
        P("groups", None),
        P("tensor", "adapter"),
        P("adapter", "tensor", None),
        P("adapter", None, None),
    )
    out_specs = P("groups", ("adapter", "tensor"))
    return jax.shard_map(
        on_device, mesh=mesh, in_specs=in_specs, out_specs=out_specs, check_vma=False
    )
```

profile of v0, /device:TPU:0, one launch (start us, length us, event | category | flops | bytes accessed | tf_op | source)
XLA Modules:
  0.0 103.9 jit_solution(16362235105522439526)
XLA Ops:
  6.5 0.0 copy-start
  6.5 0.0 copy-start.2
  6.5 0.0 all-gather.2.cloned.1.call-start
  6.5 0.7 all-gather.2.cloned.1.call-update
  7.3 0.0 reduce-scatter.2.cloned.1.call-start
  7.3 0.7 fusion.6
  8.0 0.1 reduce_window_sum.11
  8.1 1.8 %reshape.45 = bf16[1,64,8,2,512]{4,3,2,1,0:T(2,128)(2,1)S(1)} reshape(bf16[1,64,8192]{2,1,0:T(8,128)(2,1)} %param.9) | data formatting | bytes 2097152 | tf_op jit(solution)/shard_map/reshape | solution.py:38
  10.0 0.0 copy-done.2
  10.0 0.2 select_reduce_fusion
  10.2 2.3 %constant_dynamic-slice_fusion = bf16[1,64,8,1,512]{4,3,2,1,0:T(2,128)(2,1)} fusion(bf16[1,64,8,2,512]{4,3,2,1,0:T(2,128)(2,1)S(1)} %reshape.45, s32[]{:T(128)S(6)} %select_n.15), kind=kLoop, calls=%fused_computation.23 | loop fusion | bytes 1048580 | tf_op jit(solution)/shard_map/dynamic_slice | solution.py:41
  12.5 46.0 %all-gather.2.cloned.1.call-done = bf16[64,14336]{1,0:T(8,128)(2,1)} async-done(((bf16[8,14336]{1,0:T(8,128)(2,1)}), bf16[64,14336]{1,0:T(8,128)(2,1)}) %all-gather.2.cloned.1.call-update) | async-done | bytes 1835024 | tf_op jit(solution)/shard_map/all_gather | solution.py:28
  58.5 15.8 %fusion.15 = f32[64,1024]{1,0:T(8,128)} fusion(bf16[64,14336]{1,0:T(8,128)(2,1)} %all-gather.2.cloned.1.call-done, bf16[14336,1024]{1,0:T(8,128)(2,1)} %param.7), kind=kOutput, calls=%fused_computation.24 | convolution fusion | flops 1879048192 | bytes 31457280 | tf_op jit(solution)/shard_map/dot_general | solution.py:29
  74.3 0.0 reduce-scatter.2.cloned.1.call-update
  74.4 0.0 copy-done
  74.4 0.0 copy-start.1
  74.4 2.5 %fusion.3 = f32[1,16,64]{2,1,0:T(8,128)S(1)} fusion(bf16[1,14336,64]{1,2,0:T(8,128)(2,1)S(1)} %copy-done, bf16[64,14336]{1,0:T(8,128)(2,1)} %all-gather.2.cloned.1.call-done, s32[64]{0:T(128)S(1)} %multiply_add_fusion, s32[16]{0:T(128)S(1)} %iota_add_fusion), kind=kOutput, calls=%fused_computation.6 | convolution fusion | flops 58950656 | bytes 3674432 | tf_op jit(solution)/shard_map/ldm,lmu->ldu/dot_general | solution.py:32
  76.9 2.5 %psum.7 = bf16[1,16,64]{2,1,0:T(8,128)(2,1)S(1)} all-reduce(f32[1,16,64]{2,1,0:T(8,128)S(1)} %fusion.3), channel_id=1, replica_groups=mesh['groups'=2,'adapter'=8,'tensor'=2] {'tensor'}, use_global_device_ids=true, to_apply=%region_3.4 | all-reduce | flops 1024 | bytes 6144 | tf_op jit(solution)/shard_map/psum | solution.py:35
  79.3 0.0 copy-done.1
  79.3 0.7 fusion.2
  80.0 0.1 all_to_all.8
  80.1 0.5 broadcast.33
  80.6 1.4 %reduce.1 = bf16[8,8192]{1,0:T(8,128)(2,1)S(1)} reduce(bf16[8,1,8192]{2,1,0:T(2,128)(2,1)S(1)} %all_to_all.8, bf16[]{:T(256)} %broadcast.33), dimensions={1}, to_apply=%all_to_all.8.reduce_sub_computation | reduce | bytes 262146 | tf_op jit(solution)/shard_map/all_to_all | solution.py:46
  82.0 0.7 reshape.60
  82.7 3.6 %all-to-all-start = ((bf16[8,2,4096]{2,1,0:T(2,128)(2,1)}), bf16[8,2,4096]{2,1,0:T(2,128)(2,1)S(1)}, u32[]{:S(2)}, u32[]{:S(2)}) async-start(bf16[8,2,4096]{2,1,0:T(2,128)(2,1)} %reshape.60), calls=%async_computation.1 | async-start | bytes 262144 | tf_op jit(solution)/shard_map/all_to_all | solution.py:46
  86.4 7.3 %all-to-all-done = bf16[8,2,4096]{2,1,0:T(2,128)(2,1)S(1)} async-done(((bf16[8,2,4096]{2,1,0:T(2,128)(2,1)}), bf16[8,2,4096]{2,1,0:T(2,128)(2,1)S(1)}, u32[]{:S(2)}, u32[]{:S(2)}) %all-to-all-start) | async-done | bytes 131104 | tf_op jit(solution)/shard_map/all_to_all | solution.py:46
  93.7 0.1 reshape.61
  93.8 0.8 reduce
  94.6 0.1 reshape.49
  94.7 0.7 gather_fusion
  95.4 0.0 reduce-scatter.2.cloned.1.call-done
  95.4 1.6 %add_convert_fusion = bf16[64,512]{1,0:T(8,128)(2,1)} fusion(f32[64,512]{1,0:T(8,128)} %reduce-scatter.2.cloned.1.call-done, bf16[64,512]{1,0:T(8,128)(2,1)S(1)} %gather_fusion, pred[64]{0:T(512)(128)(4,1)S(1)} %get-tuple-element.5), kind=kLoop, calls=%fused_computation.8 | loop fusion | flops 131072 | bytes 262208 | tf_op jit(solution)/shard_map/convert_element_type | solution.py:51
  (4 shorter events, 0.0 us)
Async XLA Ops:
  6.5 67.8 %copy-start = (bf16[1,14336,64]{1,2,0:T(8,128)(2,1)S(1)}, bf16[1,14336,64]{1,2,0:T(8,128)(2,1)}, u32[]{:S(2)}) copy-start(bf16[1,14336,64]{1,2,0:T(8,128)(2,1)} %param.8) | copy-start | bytes 5505028
  6.5 3.5 %copy-start.2 = (s32[64,1]{0,1:T(1,128)S(1)}, s32[64,1]{0,1:T(1,128)}, u32[]{:S(2)}) copy-start(s32[64,1]{0,1:T(1,128)} %param.6) | copy-start | bytes 772
  6.5 52.0 %all-gather.2.cloned.1.call-start = ((), (), s32[]{:S(2)}) async-start(), calls=%async_computation.2 | async-start | bytes 2064384 | tf_op jit(solution)/shard_map/all_gather | solution.py:28
  7.3 88.2 %reduce-scatter.2.cloned.1.call-start = ((), (), s32[]{:S(2)}) async-start(), calls=%async_computation.3 | async-start | bytes 393216 | tf_op jit(solution)/shard_map/reduce_scatter | solution.py:50
  74.4 5.0 %copy-start.1 = (bf16[1,64,8,1,512]{4,3,2,1,0:T(2,128)(2,1)S(1)}, bf16[1,64,8,1,512]{4,3,2,1,0:T(2,128)(2,1)}, u32[]{:S(2)}) copy-start(bf16[1,64,8,1,512]{4,3,2,1,0:T(2,128)(2,1)} %constant_dynamic-slice_fusion) | copy-start | bytes 1572868
  82.7 11.0 %all-to-all-start = ((bf16[8,2,4096]{2,1,0:T(2,128)(2,1)}), bf16[8,2,4096]{2,1,0:T(2,128)(2,1)S(1)}, u32[]{:S(2)}, u32[]{:S(2)}) async-start(bf16[8,2,4096]{2,1,0:T(2,128)(2,1)} %reshape.60), calls=%async_computation.1 | async-start | bytes 262144 | tf_op jit(solution)/shard_map/all_to_all | solution.py:46
Sparse Core Ops, SparseCore 0:
  9.5 48.9 all-gather.1
  74.5 6.6 reduce-scatter.1
where the time goes:
time: 104 us
  waiting for transfers between devices  54.1 us (52%)
  matrix products  19 us (18%)
  between operations  13.5 us (13%)
  local copies, waits for them, and re-layouts  6.34 us (6%)
  other arithmetic  4.81 us (5%)
  starting transfers between devices  3.68 us (4%)
  blocking collectives  2.49 us (2%)
    all_gather x1, waiting for transfers between devices, on_device(): piece = lax.all_gather(hidden, 'adapter', axis=0, tiled=True)  46 us
    dot_general x1, matrix products, on_device(): product = jnp.dot(piece, down_matrix, preferred_element_type=jnp.float32)  15.8 us
    all_to_all x1, waiting for transfers between devices, on_device(): lax.all_to_all(produced, 'adapter', split_axis=0, concat_axis=0, tiled=True)  7.32 us
    all_to_all x1, starting transfers between devices, on_device(): lax.all_to_all(produced, 'adapter', split_axis=0, concat_axis=0, tiled=True)  3.64 us
    psum x1, blocking collectives, on_device(): reduced = lax.psum(partial_rank, 'tensor').astype(jnp.bfloat16)  2.49 us
    dot_general x1, matrix products, on_device(): jnp.einsum('ldm,lmu->ldu', selected_rows, adapter_input_factor, preferred...  2.46 us
    dynamic_slice x1, local copies, waits for them, and re-layouts, on_device(): lax.dynamic_slice_in_dim(output_factor_split, part_index, 1, 3)  2.31 us
    all_to_all x2, other arithmetic, on_device(): lax.all_to_all(produced, 'adapter', split_axis=0, concat_axis=0, tiled=True)  2.17 us
  transfers between devices with their start and end apart: 3, of which 2 were waited for; matrix products, arithmetic and copies ran while one was open for 12% of the time, Pallas kernels for 0%

commit v1 on v0

--- a/solution.py
+++ b/solution.py
@@ -1,7 +1,297 @@
+import functools
+
 import jax
 import jax.numpy as jnp
 from jax import lax
+from jax.experimental import pallas as pl
+from jax.experimental.pallas import tpu as pltpu
 from jax.sharding import PartitionSpec as P
+
+MESH = pl.DeviceIdType.MESH
+DEPTH = 1024
+SKEW = 2
+
+
+def fused_kernel(
+    n, chunks, index_ref, hidden_ref, w_ref, a_ref, b_ref, out_ref,
+    xbuf, wbuf, abuf, bbuf, acc, acc_in, low, low_in, dbuf, darr,
+    w_sem, a_sem, b_sem, right_send, right_recv, left_send, left_recv,
+    low_sem, acc_sem, d_send, d_recv,
+):
+    half = n // 2
+    me = lax.axis_index("adapter")
+    core = lax.axis_index("tensor")
+    sibling = 1 - core
+    columns = out_ref.shape[1]
+    rows = out_ref.shape[0]
+    capacity = dbuf.shape[1]
+    parity = me % 2
+    place = (1 - parity) * (me // 2) + parity * (n - 1 - me // 2)
+
+    def at_place(p):
+        p = (p + 2 * n) % n
+        upper = p // half
+        return (1 - upper) * 2 * p + upper * (2 * (n - 1 - p) + 1)
+
+    right, left = at_place(place + 1), at_place(place - 1)
+    from_left = [at_place(place - h) for h in range(half + 1)]
+    from_right = [at_place(place + h) for h in range(half + 1)]
+
+    def copy_right(c, h):
+        block = xbuf.at[c, from_left[h - 1]]
+        return pltpu.make_async_remote_copy(
+            src_ref=block, dst_ref=block, send_sem=right_send.at[c, h - 1],
+            recv_sem=right_recv.at[c, h - 1], device_id={"adapter": right}, device_id_type=MESH)
+
+    def copy_left(c, h):
+        block = xbuf.at[c, from_right[h - 1]]
+        return pltpu.make_async_remote_copy(
+            src_ref=block, dst_ref=block, send_sem=left_send.at[c, h - 1],
+            recv_sem=left_recv.at[c, h - 1], device_id={"adapter": left}, device_id_type=MESH)
+
+    def arrive_right(c, h):
+        block = xbuf.at[c, from_left[h]]
+        return pltpu.make_async_remote_copy(
+            src_ref=block, dst_ref=block, send_sem=right_send.at[c, h - 1],
+            recv_sem=right_recv.at[c, h - 1], device_id={"adapter": right}, device_id_type=MESH)
+
+    def arrive_left(c, h):
+        block = xbuf.at[c, from_right[h]]
+        return pltpu.make_async_remote_copy(
+            src_ref=block, dst_ref=block, send_sem=left_send.at[c, h - 1],
+            recv_sem=left_recv.at[c, h - 1], device_id={"adapter": left}, device_id_type=MESH)
+
+    barrier = pltpu.get_barrier_semaphore()
+    for k in range(1, n):
+        pl.semaphore_signal(
+            barrier, inc=1, device_id={"adapter": (me + k) % n}, device_id_type=MESH)
+    pl.semaphore_signal(barrier, inc=1, device_id={"tensor": sibling}, device_id_type=MESH)
+
+    def w_copy(c):
+        return pltpu.make_async_copy(
+            w_ref.at[pl.ds(pl.multiple_of(c * DEPTH, DEPTH), DEPTH), :], wbuf.at[c], w_sem.at[c])
+
+    def a_copy(c):
+        return pltpu.make_async_copy(
+            a_ref.at[0, :, pl.ds(pl.multiple_of(c * DEPTH, DEPTH), DEPTH)], abuf.at[c], a_sem.at[c])
+
+    def b_copy(k):
+        start = pl.multiple_of((2 * k + core) * columns, columns)
+        return pltpu.make_async_copy(
+            b_ref.at[0, :, pl.ds(start, columns)], bbuf.at[k], b_sem.at[k])
+
+    def start_loads(c, carry):
+        w_copy(c).start()
+        a_copy(c).start()
+        return carry
+
+    lax.fori_loop(0, chunks, start_loads, 0)
+    for k in range(n):
+        b_copy(k).start()
+
+    side = DEPTH // 2
+    for c in range(chunks):
+        part = hidden_ref[:, c * DEPTH:(c + 1) * DEPTH].astype(jnp.float32)
+        stacked = jnp.concatenate([part[:, :side], part[:, side:]], axis=0)
+        xbuf[c, me] = stacked.astype(jnp.bfloat16)
+    acc[...] = jnp.zeros_like(acc)
+    low[...] = jnp.zeros_like(low)
+
+    idents = index_ref[...]
+    onehot = (lax.broadcasted_iota(jnp.int32, (n, rows), 0) == idents).astype(jnp.float32)
+    earlier = (
+        lax.broadcasted_iota(jnp.int32, (rows, rows), 0)
+        < lax.broadcasted_iota(jnp.int32, (rows, rows), 1)
+    ).astype(jnp.bfloat16)
+    running = jnp.dot(onehot.astype(jnp.bfloat16), earlier, preferred_element_type=jnp.float32)
+    ranking = jnp.sum(onehot * running, axis=0, keepdims=True)
+    slots = idents * capacity + ranking.astype(jnp.int32)
+    selector = (
+        lax.broadcasted_iota(jnp.int32, (capacity, rows), 0) + me * capacity == slots
+    ).astype(jnp.float32).astype(jnp.bfloat16)
+    placing = (
+        lax.broadcasted_iota(jnp.int32, (n * capacity, rows), 0) == slots
+    ).astype(jnp.float32)
+    placing = placing.T.astype(jnp.bfloat16)
+
+    pl.semaphore_wait(barrier, n)
+
+    low_copy = pltpu.make_async_remote_copy(
+        src_ref=low, dst_ref=low_in, send_sem=low_sem.at[0], recv_sem=low_sem.at[1],
+        device_id={"tensor": sibling}, device_id_type=MESH)
+    acc_copy = pltpu.make_async_remote_copy(
+        src_ref=acc.at[sibling], dst_ref=acc_in, send_sem=acc_sem.at[0], recv_sem=acc_sem.at[1],
+        device_id={"tensor": sibling}, device_id_type=MESH)
+
+    def step(tau, carry):
+        @pl.when(tau < chunks)
+        def _():
+            copy_right(tau, 1).start()
+            copy_left(tau, 1).start()
+
+        for h in range(1, half):
+            c = tau - SKEW * h
+
+            @pl.when((c >= 0) & (c < chunks))
+            def _(c=c, h=h):
+                arrive_right(c, h).wait_recv()
+                if h + 1 < half:
+                    copy_right(c, h + 1).start()
+                else:
+                    @pl.when(c % 2 == 0)
+                    def _():
+                        copy_right(c, h + 1).start()
+                arrive_left(c, h).wait_recv()
+                if h + 1 < half:
+                    copy_left(c, h + 1).start()
+                else:
+                    @pl.when(c % 2 == 1)
+                    def _():
+                        copy_left(c, h + 1).start()
+
+        c = tau - SKEW * half
+
+        @pl.when(c >= 0)
+        def _():
+            @pl.when(c % 2 == 0)
+            def _():
+                arrive_right(c, half).wait_recv()
+
+            @pl.when(c % 2 == 1)
+            def _():
+                arrive_left(c, half).wait_recv()
+
+            a_copy(c).wait()
+            w_copy(c).wait()
+            pairs = xbuf[c].astype(jnp.float32).reshape(n, 2, rows // n, side)
+            x = jnp.concatenate(
+                [pairs[:, 0].reshape(rows, side), pairs[:, 1].reshape(rows, side)], axis=1
+            ).astype(jnp.bfloat16)
+            low[...] += lax.dot_general(
+                x, abuf[c], (((1,), (1,)), ((), ())), preferred_element_type=jnp.float32)
+
+            @pl.when(c == chunks - 1)
+            def _():
+                low_copy.start()
+
+            for which in (sibling, core):
+                start = pl.multiple_of(which * columns, columns)
+                acc[which] += jnp.dot(
+                    x, wbuf[c, :, pl.ds(start, columns)], preferred_element_type=jnp.float32)
+                if which is sibling:
+                    @pl.when(c == chunks - 1)
+                    def _():
+                        acc_copy.start()
+
+        return carry
+
+    lax.fori_loop(0, chunks + SKEW * half, step, 0)
+
+    low_copy.wait()
+    reduced = (low[...] + low_in[...]).astype(jnp.bfloat16)
+    chosen = jnp.dot(selector, reduced, preferred_element_type=jnp.float32).astype(jnp.bfloat16)
+    for k in range(n):
+        b_copy(k).wait()
+
+    def d_copy(k):
+        return pltpu.make_async_remote_copy(
+            src_ref=dbuf.at[k], dst_ref=darr.at[me], send_sem=d_send.at[k],
+            recv_sem=d_recv.at[k], device_id={"adapter": (me + k) % n}, device_id_type=MESH)
+
+    def d_arrive(k):
+        return pltpu.make_async_remote_copy(
+            src_ref=dbuf.at[k], dst_ref=darr.at[(me + n - k) % n], send_sem=d_send.at[k],
+            recv_sem=d_recv.at[k], device_id={"adapter": (me + k) % n}, device_id_type=MESH)
+
+    for k in range(1, n):
+        dbuf[k] = jnp.dot(
+            chosen, bbuf[(me + k) % n], preferred_element_type=jnp.float32
+        ).astype(jnp.bfloat16)
+        d_copy(k).start()
+    darr[me] = jnp.dot(chosen, bbuf[me], preferred_element_type=jnp.float32).astype(jnp.bfloat16)
+
+    acc_copy.wait()
+    acc_in[...] += acc[core]
+    for k in range(1, n):
+        d_arrive(k).wait_recv()
+    delta = jnp.dot(
+        placing, darr[...].reshape(n * capacity, columns), preferred_element_type=jnp.float32)
+    out_ref[...] = (acc_in[...] + delta).astype(out_ref.dtype)
+
+    for k in range(1, n):
+        d_copy(k).wait_send()
+
+    def finish(c, carry):
+        for h in range(1, half):
+            copy_right(c, h).wait_send()
+            copy_left(c, h).wait_send()
+
+        @pl.when(c % 2 == 0)
+        def _():
+            copy_right(c, half).wait_send()
+
+        @pl.when(c % 2 == 1)
+        def _():
+            copy_left(c, half).wait_send()
+
+        return carry
+
+    lax.fori_loop(0, chunks, finish, 0)
+
+
+def fits(hidden, row_adapter_index, down_matrix, adapter_input_factor):
+    n, cores = lax.axis_size("adapter"), lax.axis_size("tensor")
+    count, inner, width = adapter_input_factor.shape
+    columns = down_matrix.shape[1]
+    return (
+        n % 2 == 0 and n >= 4 and cores == 2 and count == 1 and hidden.shape[0] == 8
+        and row_adapter_index.shape[0] == 8 * n and inner % DEPTH == 0
+        and columns % (cores * 128) == 0 and down_matrix.size <= 16 * 1024 * 1024
+    )
+
+
+def fused(hidden, row_adapter_index, down_matrix, adapter_input_factor, adapter_output_factor):
+    n = lax.axis_size("adapter")
+    rows = row_adapter_index.shape[0]
+    capacity = 2 * (rows // n)
+    inner, columns = down_matrix.shape
+    width = adapter_input_factor.shape[2]
+    mine = columns // 2
+    chunks = inner // DEPTH
+    half = n // 2
+    bf16, f32 = jnp.bfloat16, jnp.float32
+    vmem = pl.BlockSpec(memory_space=pltpu.VMEM)
+    anywhere = pl.BlockSpec(memory_space=pl.ANY)
+    dma = pltpu.SemaphoreType.DMA
+    return pl.pallas_call(
+        functools.partial(fused_kernel, n, chunks),
+        out_shape=jax.ShapeDtypeStruct((rows, mine), bf16),
+        in_specs=[vmem, vmem, anywhere, anywhere, anywhere],
+        out_specs=vmem,
+        scratch_shapes=[
+            pltpu.VMEM((chunks, n, 16, DEPTH // 2), bf16),
+            pltpu.VMEM((chunks, DEPTH, columns), bf16),
+            pltpu.VMEM((chunks, width, DEPTH), bf16),
+            pltpu.VMEM((n, width, mine), bf16),
+            pltpu.VMEM((2, rows, mine), f32),
+            pltpu.VMEM((rows, mine), f32),
+            pltpu.VMEM((rows, width), f32),
+            pltpu.VMEM((rows, width), f32),
+            pltpu.VMEM((n, capacity, mine), bf16),
+            pltpu.VMEM((n, capacity, mine), bf16),
+            dma((chunks,)), dma((chunks,)), dma((n,)),
+            dma((chunks, half)), dma((chunks, half)), dma((chunks, half)), dma((chunks, half)),
+            dma((2,)), dma((2,)), dma((n,)), dma((n,)),
+        ],
+        compiler_params=pltpu.CompilerParams(
+            collective_id=0, has_side_effects=True, vmem_limit_bytes=56 * 1024 * 1024),
+        cost_estimate=pl.CostEstimate(
+            flops=2 * rows * inner * (columns + width),
+            bytes_accessed=2 * inner * (columns + width), transcendentals=0),
+    )(
+        row_adapter_index.reshape(1, rows), hidden, down_matrix,
+        jnp.swapaxes(adapter_input_factor, 1, 2), adapter_output_factor,
+    )
 
 
 def slot_table(row_adapter_index, capacity, adapters):
@@ -15,6 +305,9 @@
 def on_device(hidden, row_adapter_index, down_matrix, adapter_input_factor, adapter_output_factor):
     adapter_count = lax.axis_size("adapter")
     tensor_count = lax.axis_size("tensor")
+    if fits(hidden, row_adapter_index, down_matrix, adapter_input_factor):
+        return fused(
+            hidden, row_adapter_index, down_matrix, adapter_input_factor, adapter_output_factor)
     local_row_count, inner_product, adapter_rank_width = adapter_input_factor.shape
     adapters = local_row_count * adapter_count
     rows_total = row_adapter_index.shape[0]

time: 104 us -> 47.3 us (0.45)
  waiting for transfers between devices: 54.1 us -> 0 us
  Pallas kernels: 0 us -> 45.6 us
  matrix products: 19 us -> 0 us
  between operations: 13.5 us -> 0.01 us
  local copies, waits for them, and re-layouts: 6.34 us -> 1.47 us
  other arithmetic: 4.81 us -> 0 us
  starting transfers between devices: 3.68 us -> 0 us
  blocking collectives: 2.49 us -> 0 us
    all_gather x1 -> x0, waiting for transfers between devices: 46 us -> none  [on_device(): piece = lax.all_gather(hidden, 'adapter', axis=0, tiled=True)]
    pallas_call x0 -> x1, Pallas kernels: none -> 45.6 us  [fused(): pl.pallas_call(functools.partial(fused_kernel, n, chunks), out_shape=jax....]
    dot_general x3 -> x0, matrix products: 19 us -> none  [the longest x1 15.8 us: on_device(): product = jnp.dot(piece, down_matrix, preferred_element_type=jnp.float32)]
    all_to_all x1 -> x0, waiting for transfers between devices: 7.32 us -> none  [on_device(): lax.all_to_all(produced, 'adapter', split_axis=0, concat_axis=0, tiled=True)]
    all_to_all x1 -> x0, starting transfers between devices: 3.64 us -> none  [on_device(): lax.all_to_all(produced, 'adapter', split_axis=0, concat_axis=0, tiled=True)]
    psum x1 -> x0, blocking collectives: 2.49 us -> none  [on_device(): reduced = lax.psum(partial_rank, 'tensor').astype(jnp.bfloat16)]
    convert_element_type x2 -> x0, other arithmetic: 2.35 us -> none  [the longest x1 1.62 us: on_device(): return (summed + delta.astype(jnp.float32)).astype(jnp.bfloat16)]
    dynamic_slice x1 -> x0, local copies, waits for them, and re-layouts: 2.31 us -> none  [on_device(): lax.dynamic_slice_in_dim(output_factor_split, part_index, 1, 3)]
  transfers between devices with their start and end apart: 3 -> 0, of which waited for: 2 -> 0; matrix products, arithmetic and copies ran while one was open for 12% -> 0% of each run, Pallas kernels for 0% -> 0%
where the time goes in v1:
time: 47.3 us; the launch traced here: 47.1 us
  Pallas kernels  45.6 us (96%)
  local copies, waits for them, and re-layouts  1.47 us (3%)
    pallas_call x1, Pallas kernels, fused(): pl.pallas_call(functools.partial(fused_kernel, n, chunks), out_shape=jax....  45.6 us
    unnamed x1, local copies, waits for them, and re-layouts  1.47 us

profile of v1, /device:TPU:0, one launch (start us, length us, event | category | flops | bytes accessed | tf_op | source)
XLA Modules:
  0.0 47.1 jit_solution(2324207921486459720)
XLA Ops:
  0.0 45.6 %shard_map.55 = bf16[64,512]{1,0:T(8,128)(2,1)} custom-call(s32[1,64]{1,0:T(1,128)} %bitcast.3, bf16[8,14336]{1,0:T(8,128)(2,1)} %hidden_ref.1, bf16[14336,1024]{1,0:T(8,128)(2,1)} %w_ref.1, bf16[1,64,14336]{2,1,0:T(8,128)(2,1)} %bitcast.2, bf16[1,64,8192]{2,1,0:T(8,128)(2,1)} %b_ref.1), custom_call_target="tpu_custom_call" | custom-call | flops 1996488704 | bytes 31195136 | tf_op jit(solution)/shard_map/pallas_call | solution.py:266
  45.6 1.5 %copy.7 = bf16[64,512]{1,0:T(8,128)(2,1)} copy(bf16[64,512]{1,0:T(8,128)(2,1)} %shard_map.55) | data formatting | bytes 131072

commit v2 on v1

--- a/solution.py
+++ b/solution.py
@@ -8,15 +8,15 @@
 from jax.sharding import PartitionSpec as P
 
 MESH = pl.DeviceIdType.MESH
-DEPTH = 1024
+DEPTH = 3584
 SKEW = 2
 
 
 def fused_kernel(
-    n, chunks, index_ref, hidden_ref, w_ref, a_ref, b_ref, out_ref,
-    xbuf, wbuf, abuf, bbuf, acc, acc_in, low, low_in, dbuf, darr,
+    n, chunks, index_hbm, hidden_hbm, w_ref, a_ref, b_ref, out_ref,
+    hidden_ref, index_ref, xbuf, wbuf, abuf, bbuf, acc, acc_in, low, low_in, dbuf, darr,
     w_sem, a_sem, b_sem, right_send, right_recv, left_send, left_recv,
-    low_sem, acc_sem, d_send, d_recv,
+    low_sem, acc_sem, d_send, d_recv, in_sem,
 ):
     half = n // 2
     me = lax.axis_index("adapter")
@@ -80,23 +80,36 @@
         return pltpu.make_async_copy(
             b_ref.at[0, :, pl.ds(start, columns)], bbuf.at[k], b_sem.at[k])
 
-    def start_loads(c, carry):
-        w_copy(c).start()
-        a_copy(c).start()
-        return carry
-
-    lax.fori_loop(0, chunks, start_loads, 0)
-    for k in range(n):
-        b_copy(k).start()
+    hidden_copy = pltpu.make_async_copy(hidden_hbm, hidden_ref, in_sem.at[0])
+    index_copy = pltpu.make_async_copy(index_hbm, index_ref, in_sem.at[1])
+    hidden_copy.start()
+    index_copy.start()
+    hidden_copy.wait()
 
     side = DEPTH // 2
     for c in range(chunks):
         part = hidden_ref[:, c * DEPTH:(c + 1) * DEPTH].astype(jnp.float32)
         stacked = jnp.concatenate([part[:, :side], part[:, side:]], axis=0)
         xbuf[c, me] = stacked.astype(jnp.bfloat16)
+
+    pl.semaphore_wait(barrier, n)
+    for c in range(SKEW):
+        copy_right(c, 1).start()
+        copy_left(c, 1).start()
+
+    def start_loads(c, carry):
+        w_copy(c).start()
+        a_copy(c).start()
+        return carry
+
+    lax.fori_loop(0, chunks, start_loads, 0)
+    for k in range(n):
+        b_copy(k).start()
+
     acc[...] = jnp.zeros_like(acc)
     low[...] = jnp.zeros_like(low)
 
+    index_copy.wait()
     idents = index_ref[...]
     onehot = (lax.broadcasted_iota(jnp.int32, (n, rows), 0) == idents).astype(jnp.float32)
     earlier = (
@@ -114,8 +127,6 @@
     ).astype(jnp.float32)
     placing = placing.T.astype(jnp.bfloat16)
 
-    pl.semaphore_wait(barrier, n)
-
     low_copy = pltpu.make_async_remote_copy(
         src_ref=low, dst_ref=low_in, send_sem=low_sem.at[0], recv_sem=low_sem.at[1],
         device_id={"tensor": sibling}, device_id_type=MESH)
@@ -185,7 +196,7 @@
 
         return carry
 
-    lax.fori_loop(0, chunks + SKEW * half, step, 0)
+    lax.fori_loop(SKEW, chunks + SKEW * half, step, 0)
 
     low_copy.wait()
     reduced = (low[...] + low_in[...]).astype(jnp.bfloat16)
@@ -203,7 +214,7 @@
             src_ref=dbuf.at[k], dst_ref=darr.at[(me + n - k) % n], send_sem=d_send.at[k],
             recv_sem=d_recv.at[k], device_id={"adapter": (me + k) % n}, device_id_type=MESH)
 
-    for k in range(1, n):
+    for k in sorted(range(1, n), key=lambda k: -min(k, n - k)):
         dbuf[k] = jnp.dot(
             chosen, bbuf[(me + k) % n], preferred_element_type=jnp.float32
         ).astype(jnp.bfloat16)
@@ -266,9 +277,11 @@
     return pl.pallas_call(
         functools.partial(fused_kernel, n, chunks),
         out_shape=jax.ShapeDtypeStruct((rows, mine), bf16),
-        in_specs=[vmem, vmem, anywhere, anywhere, anywhere],
+        in_specs=[anywhere] * 5,
         out_specs=vmem,
         scratch_shapes=[
+            pltpu.VMEM(hidden.shape, bf16),
+            pltpu.VMEM((1, rows), jnp.int32),
             pltpu.VMEM((chunks, n, 16, DEPTH // 2), bf16),
             pltpu.VMEM((chunks, DEPTH, columns), bf16),
             pltpu.VMEM((chunks, width, DEPTH), bf16),
@@ -281,7 +294,7 @@
             pltpu.VMEM((n, capacity, mine), bf16),
             dma((chunks,)), dma((chunks,)), dma((n,)),
             dma((chunks, half)), dma((chunks, half)), dma((chunks, half)), dma((chunks, half)),
-            dma((2,)), dma((2,)), dma((n,)), dma((n,)),
+            dma((2,)), dma((2,)), dma((n,)), dma((n,)), dma((2,)),
         ],
         compiler_params=pltpu.CompilerParams(
             collective_id=0, has_side_effects=True, vmem_limit_bytes=56 * 1024 * 1024),

time: 47.3 us -> 38.1 us (0.81)
  Pallas kernels: 45.6 us -> 36.5 us
    pallas_call x1, Pallas kernels: 45.6 us -> 36.5 us  [fused(): pl.pallas_call(functools.partial(fused_kernel, n, chunks), out_shape=jax....]
where the time goes in v2:
time: 38.1 us; the launch traced here: 38 us
  Pallas kernels  36.5 us (96%)
  local copies, waits for them, and re-layouts  1.47 us (4%)
    pallas_call x1, Pallas kernels, fused(): pl.pallas_call(functools.partial(fused_kernel, n, chunks), out_shape=jax....  36.5 us
    unnamed x1, local copies, waits for them, and re-layouts  1.47 us

profile of v2, /device:TPU:0, one launch (start us, length us, event | category | flops | bytes accessed | tf_op | source)
XLA Modules:
  0.0 38.0 jit_solution(17857302942775089307)
XLA Ops:
  0.0 36.5 %shard_map.55 = bf16[64,512]{1,0:T(8,128)(2,1)} custom-call(s32[1,64]{1,0:T(1,128)} %bitcast.3, bf16[8,14336]{1,0:T(8,128)(2,1)} %hidden_hbm.1, bf16[14336,1024]{1,0:T(8,128)(2,1)} %w_ref.1, bf16[1,64,14336]{2,1,0:T(8,128)(2,1)} %bitcast.2, bf16[1,64,8192]{2,1,0:T(8,128)(2,1)} %b_ref.1), custom_call_target="tpu_custom_call" | custom-call | flops 1996488704 | bytes 31195136 | tf_op jit(solution)/shard_map/pallas_call | solution.py:277
  36.5 1.5 %copy.7 = bf16[64,512]{1,0:T(8,128)(2,1)} copy(bf16[64,512]{1,0:T(8,128)(2,1)} %shard_map.55) | data formatting | bytes 131072
